TPU v7x, 32 devices: a whole 2x2x4 slice. The times are simulated.
32 devices in a mesh: dp: 2 (over x), expert: 8 (over z, core), tensor: 2 (over y).
Axes of the slice: x: 2, y: 2, z: 4, core: 2. Of those that a mesh axis runs over, the one named last changes fastest.
Arguments:
- tokens: bfloat16 [256, 2048], P(('dp', 'expert')), may hold values from -6 to 6
- routes: int32 [256, 8], P(('dp', 'expert')), may hold values from 0 to 15, all different within a row; in each aligned block of 16 rows (0 to 15, 16 to 31, ...) at most 16 rows name the same one
- route_weight: float32 [256, 8], P(('dp', 'expert')), may hold values from 0.02 to 0.5
- weights_gate_up: bfloat16 [16, 2048, 2, 768], P('expert', None, None, 'tensor'), may hold values from -0.125 to 0.125
- weights_down: bfloat16 [16, 2048, 768], P('expert', None, 'tensor'), may hold values from -0.21875 to 0.21875
- cotangent: bfloat16 [256, 2048], P(('dp', 'expert')), may hold values from -6 to 6
Outputs:
- layer_out: bfloat16 [256, 2048], P(('dp', 'expert'), 'tensor')
- tokens_grad: bfloat16 [256, 2048], P(('dp', 'expert'), 'tensor')
- gate_up_grad: bfloat16 [16, 2048, 2, 768], P('expert', 'dp', None, 'tensor')
- down_grad: bfloat16 [16, 2048, 768], P('expert', 'dp', 'tensor')
Inputs may be any that keep to these rules, and one draw needn't show every extreme that they name: `routes`: each row names 8 different experts. Among the 16 rows of one index of dp and expert no expert is named more than 16 times, a bound that some block reaches.
All inputs are finite; a program needn't handle non-finite values.
Results may differ from a plain program's by a relative error of at most 0.0072.
Values may be sent and summed in bfloat16 or wider, within the bound.
A program may use at most 64 MiB of HBM per device.

v0:
```python
import jax
import jax.numpy as jnp
from jax import lax
from jax.sharding import PartitionSpec as P

F32 = jnp.float32
BF16 = jnp.bfloat16


def cut(value):
    return lax.reduce_precision(value, exponent_bits=8, mantissa_bits=7)


def body(tokens, routes, route_weight, weights_gate_up, weights_down, cotangent):
    tok_rows, width = tokens.shape
    expert_local = weights_gate_up.shape[0]
    n_expert = lax.axis_size("expert")
    n_tensor = lax.axis_size("tensor")
    n_dp = lax.axis_size("dp")
    expert_total = expert_local * n_expert
    group = tok_rows * n_expert
    my_dp = lax.axis_index("dp")
    chosen = routes[:, :, None] == jnp.arange(expert_total, dtype=jnp.int32)[None, None, :]
    dense = jnp.sum(jnp.where(chosen, route_weight[:, :, None], 0.0), axis=1)
    first = cut(dense)
    second = cut(dense - first)
    third = dense - first - second
    parts = jnp.concatenate([first, second, third], axis=1).astype(BF16)
    spare = -parts.shape[1] % 128
    parts = jnp.pad(parts, ((0, 0), (0, spare)))
    sent = jnp.concatenate([tokens, cotangent, parts], axis=1)
    held = lax.all_gather(sent, "expert", axis=0, tiled=True)
    tok = held[:, :width]
    cot = held[:, width : 2 * width]
    parts = held[:, 2 * width : 2 * width + 3 * expert_total].astype(F32)
    parts = parts.reshape(group, 3, expert_total)
    weight = parts[:, 0] + parts[:, 1] + parts[:, 2]
    weight = lax.dynamic_slice_in_dim(
        weight, lax.axis_index("expert") * expert_local, expert_local, axis=1
    ).T[:, :, None]
    share = width // n_dp

    def columns(shift):
        start = lax.rem(my_dp + shift, n_dp) * share
        return jnp.concatenate(
            [
                lax.dynamic_slice_in_dim(tok, start, share, axis=1),
                lax.dynamic_slice_in_dim(cot, start, share, axis=1),
            ],
            axis=1,
        )

    def moved(value, shift):
        return lax.ppermute(value, "dp", [(i, (i + shift) % n_dp) for i in range(n_dp)])

    sides = [columns(0)] + [moved(columns(s), s) for s in range(1, n_dp)]
    gate_up = jnp.einsum("td,edgh->etgh", tok, weights_gate_up, preferred_element_type=F32)
    gate_pre = gate_up[:, :, 0, :]
    up_pre = gate_up[:, :, 1, :]
    sig_gate = jax.nn.sigmoid(gate_pre)
    silu_gate = gate_pre * sig_gate
    hidden = (silu_gate * up_pre * weight).astype(BF16)
    hidden_grad = weight * jnp.einsum("td,edh->eth", cot, weights_down, preferred_element_type=F32)
    gate_grad = (hidden_grad * up_pre * sig_gate * (1.0 + gate_pre * (1.0 - sig_gate))).astype(BF16)
    up_grad = (hidden_grad * silu_gate).astype(BF16)
    mine = jnp.stack([gate_grad, up_grad, hidden], axis=0)
    acts = jnp.concatenate([mine] + [moved(mine, s) for s in range(1, n_dp)], axis=2)
    pre_grads = jnp.stack([gate_grad, up_grad], axis=2)
    out_part = jnp.sum(
        jnp.einsum("eth,edh->etd", hidden, weights_down, preferred_element_type=F32), axis=0
    ).astype(BF16)
    in_part = jnp.sum(
        jnp.einsum("etgh,edgh->etd", pre_grads, weights_gate_up, preferred_element_type=F32), axis=0
    ).astype(BF16)
    both = jnp.stack([out_part, in_part]).reshape(
        2, n_expert, tok_rows, n_tensor, width // n_tensor
    )
    both = both.transpose(1, 3, 0, 2, 4).reshape(
        n_expert * n_tensor, 2, tok_rows, width // n_tensor
    )
    back = lax.all_to_all(both, ("expert", "tensor"), split_axis=0, concat_axis=0, tiled=True)
    results = jnp.sum(back.astype(F32), axis=0).astype(BF16)
    rows = jnp.concatenate(sides, axis=0)
    gate_up_grad = jnp.einsum(
        "td,geth->edgh", rows[:, :share], acts[:2], preferred_element_type=F32
    ).astype(BF16)
    down_grad = jnp.einsum(
        "td,eth->edh", rows[:, share:], acts[2], preferred_element_type=F32
    ).astype(BF16)
    return (results[0], results[1], gate_up_grad, down_grad)


def solution(mesh):
    return jax.shard_map(
        body,
        mesh=mesh,
        in_specs=(
            P(("dp", "expert"), None),
            P(("dp", "expert"), None),
            P(("dp", "expert"), None),
            P("expert", None, None, "tensor"),
            P("expert", None, "tensor"),
            P(("dp", "expert"), None),
        ),
        out_specs=(
            P(("dp", "expert"), "tensor"),
            P(("dp", "expert"), "tensor"),
            P("expert", "dp", None, "tensor"),
            P("expert", "dp", "tensor"),
        ),
        check_vma=False,
    )
```

profile of v0, /device:TPU:0, one launch (start us, length us, event | category | flops | bytes accessed | tf_op | source)
XLA Modules:
  0.0 121.2 jit_solution(4500048296995259462)
XLA Ops:
  7.2 0.0 copy-start
  7.2 0.0 all-gather.2.cloned.1.call-start
  7.2 0.9 copy.62
  8.1 0.8 copy.63
  8.9 0.1 select_reduce_fusion
  9.0 0.1 fusion.56
  9.1 1.5 %pad_maximum_fusion.4 = bf16[16,4224]{1,0:T(8,128)(2,1)} fusion(bf16[16,128]{1,0:T(8,128)(2,1)S(1)} %fusion.56, bf16[16,2048]{1,0:T(8,128)(2,1)} %param.11, bf16[16,2048]{1,0:T(8,128)(2,1)} %param.6), kind=kLoop, calls=%fused_computation.63 | loop fusion | flops 405504 | bytes 270336 | tf_op jit(solution)/shard_map/concatenate | solution.py:31
  10.6 0.0 all-gather.2.cloned.1.call-update
  10.7 25.1 %all-gather.2.cloned.1.call-done = bf16[128,4224]{1,0:T(8,128)(2,1)} async-done(((bf16[16,4224]{1,0:T(8,128)(2,1)}), bf16[128,4224]{1,0:T(8,128)(2,1)}) %all-gather.2.cloned.1.call-update) | async-done | bytes 1081360 | tf_op jit(solution)/shard_map/all_gather | solution.py:32
  35.8 0.8 slice.59
  36.6 0.1 copy.80
  36.7 4.0 %fusion.12 = f32[2,128,2,384]{3,1,2,0:T(8,128)S(1)} fusion(bf16[2,2048,2,384]{3,2,1,0:T(2,128)(2,1)} %param.9, bf16[128,4224]{1,0:T(8,128)(2,1)} %all-gather.2.cloned.1.call-done), kind=kOutput, calls=%fused_computation.11 | convolution fusion | flops 805306368 | bytes 7602176 | tf_op jit(solution)/shard_map/td,edgh->etgh/dot_general | solution.py:57
  40.7 0.0 copy-start.4
  40.7 0.9 copy-done.4
  41.5 0.0 copy-done
  41.5 2.0 %fusion.7 = bf16[128,2048]{1,0:T(8,128)(2,1)} fusion(bf16[2,2048,384]{2,1,0:T(8,128)(2,1)S(1)} %copy-done, f32[2,128,2,384]{3,1,2,0:T(8,128)S(1)} %fusion.12, f32[2,128]{1,0:T(2,128)S(1)} %fusion.58), kind=kOutput, calls=%fused_computation.7 | convolution fusion | flops 403603456 | bytes 4457472 | tf_op jit(solution)/shard_map/eth,edh->etd/dot_general | solution.py:70
  43.5 2.2 %stack.28 = bf16[1,8,16,2,1024]{4,3,2,1,0:T(2,128)(2,1)} reshape(bf16[128,2048]{1,0:T(8,128)(2,1)} %fusion.7) | data formatting | bytes 1048576 | tf_op jit(solution)/shard_map/stack | solution.py:75
  45.7 2.0 %copy.68 = bf16[1,8,16,2,1024]{4,2,0,3,1:T(8,128)(2,1)} copy(bf16[1,8,16,2,1024]{4,3,2,1,0:T(2,128)(2,1)} %stack.28) | data formatting | bytes 1048576 | tf_op jit(solution)/shard_map/stack | solution.py:75
  47.7 1.9 %fusion.44 = (bf16[2,128,384]{2,1,0:T(8,128)(2,1)S(1)}, bf16[2,128,384]{2,1,0:T(8,128)(2,1)S(1)}) fusion(f32[2,128,2,384]{3,1,2,0:T(8,128)} %copy-done.4, bf16[2,2048,384]{2,1,0:T(8,128)(2,1)S(1)} %copy-done, bf16[128,4224]{1,0:T(8,128)(2,1)} %all-gather.2.cloned.1.call-done, f32[2,128]{1,0:T(2,128)S(1)} %fusion.58), kind=kOutput, calls=%fused_computation.54 | convolution fusion | flops 404029440 | bytes 4850688 | tf_op jit(solution)/shard_map/td,edh->eth/dot_general | solution.py:63
  49.7 0.0 copy-start.2
  49.7 0.7 copy-done.2
  50.4 5.8 %fusion.8 = bf16[128,2048]{1,0:T(8,128)(2,1)} fusion(bf16[2,2048,2,384]{3,2,1,0:T(2,128)(2,1)} %param.9, bf16[2,128,1,384]{3,1,0,2:T(8,128)(2,1)S(1)} %bitcast.126, bf16[2,128,1,384]{3,1,0,2:T(8,128)(2,1)S(1)} %bitcast.122), kind=kOutput, calls=%fused_computation.8 | convolution fusion | flops 805765120 | bytes 7208960 | tf_op jit(solution)/shard_map/etgh,edgh->etd/dot_general | solution.py:73
  56.2 2.2 %stack.32 = bf16[1,8,16,2,1024]{4,3,2,1,0:T(2,128)(2,1)} reshape(bf16[128,2048]{1,0:T(8,128)(2,1)} %fusion.8) | data formatting | bytes 1048576 | tf_op jit(solution)/shard_map/stack | solution.py:75
  58.4 1.2 copy.69
  59.6 2.1 %pad_maximum_fusion = bf16[2,8,16,2,1024]{4,2,0,3,1:T(8,128)(2,1)} fusion(bf16[1,8,16,2,1024]{4,2,0,3,1:T(8,128)(2,1)S(1)} %copy.69, bf16[1,8,16,2,1024]{4,2,0,3,1:T(8,128)(2,1)} %copy.68), kind=kLoop, calls=%fused_computation.21 | loop fusion | flops 524288 | bytes 2097152 | tf_op jit(solution)/shard_map/stack | solution.py:75
  61.7 4.4 %all-to-all-start = ((bf16[16,2,16,1024]{3,2,1,0:T(8,128)(2,1)}), bf16[16,2,16,1024]{3,2,1,0:T(8,128)(2,1)}, u32[]{:S(2)}, u32[]{:S(2)}) async-start(bf16[16,2,16,1024]{3,2,1,0:T(8,128)(2,1)} %bitcast.121), calls=%async_computation | async-start | bytes 2097152 | tf_op jit(solution)/shard_map/all_to_all | solution.py:81
  66.1 0.0 copy-start.5
  66.2 1.3 %fusion.66 = (bf16[128,2048]{1,0:T(8,128)(2,1)S(1)}, bf16[128,2048]{1,0:T(8,128)(2,1)S(1)}) fusion(bf16[128,4224]{1,0:T(8,128)(2,1)} %all-gather.2.cloned.1.call-done), kind=kLoop, calls=%fused_computation.95 | loop fusion | bytes 2097152 | tf_op jit(solution)/shard_map/slice | solution.py:33
  67.5 0.0 copy-start.3
  67.5 0.1 constant_dynamic-slice_fusion.4
  67.7 1.5 %collective-permute-start.1 = (bf16[128,2048]{1,0:T(8,128)(2,1)S(1)}, bf16[128,2048]{1,0:T(8,128)(2,1)S(1)}, u32[]{:S(2)}, u32[]{:S(2)}) collective-permute-start(bf16[128,2048]{1,0:T(8,128)(2,1)S(1)} %pad_maximum_fusion.3), channel_id=1, source_target_pairs={{0,16},{16,0},{1,17},{17,1},{2,18},{18,2},{3,19},{19,3},{4,20},{20... | collective-permute-start | bytes 1572872 | tf_op jit(solution)/shard_map/ppermute | solution.py:54
  69.2 0.0 copy-done.5
  69.2 0.1 fusion.48
  69.3 0.0 copy-done.3
  69.3 0.1 pad_maximum_fusion.2
  69.4 0.6 collective-permute-start
  70.1 12.4 %collective-permute-done.1 = bf16[128,2048]{1,0:T(8,128)(2,1)S(1)} collective-permute-done((bf16[128,2048]{1,0:T(8,128)(2,1)S(1)}, bf16[128,2048]{1,0:T(8,128)(2,1)S(1)}, u32[]{:S(2)}, u32[]{:S(2)}) %collective-permute-start.1) | collective-permute-done | bytes 524320 | tf_op jit(solution)/shard_map/ppermute | solution.py:54
  82.5 0.1 pad_maximum_fusion.1
  82.6 0.0 copy-start.1
  82.6 12.0 %collective-permute-done = bf16[3,2,128,384]{3,2,1,0:T(8,128)(2,1)S(1)} collective-permute-done((bf16[3,2,128,384]{3,2,1,0:T(8,128)(2,1)S(1)}, bf16[3,2,128,384]{3,2,1,0:T(8,128)(2,1)S(1)}, u32[]{:S(2)}, u32[]{:S(2)}) %collective-permute-start) | collective-permute-done | bytes 589856 | tf_op jit(solution)/shard_map/ppermute | solution.py:54
  94.6 0.8 copy-done.6
  95.4 1.8 %fusion.11 = bf16[2,1024,384]{1,2,0:T(8,128)(2,1)} fusion(bf16[256,2048]{1,0:T(8,128)(2,1)S(1)} %pad_maximum_fusion.1, bf16[3,2,128,384]{3,2,1,0:T(8,128)(2,1)S(1)} %collective-permute-done, bf16[1,2,128,384]{3,2,1,0:T(8,128)(2,1)S(1)} %fusion.48, bf16[1,2,128,384]{3,2,1,0:T(8,128)(2,1)S(1)} %bitcast.129, bf16[1,2,128,384]{3,2,1,0:T(8,128)(2,1)S(1)} %bitcast.124), kind=kOutput, calls=%fused_computation.10 | convolution fusion | flops 405012480 | bytes 3276800 | tf_op jit(solution)/shard_map/td,eth->edh/dot_general | solution.py:87
  97.1 2.6 %copy.73 = bf16[2,1024,384]{2,1,0:T(8,128)(2,1)} copy(bf16[2,1024,384]{1,2,0:T(8,128)(2,1)} %fusion.11) | data formatting | bytes 3145728
  99.7 3.9 %convert_bitcast_fusion = bf16[2,1024,2,384]{1,3,0,2:T(8,128)(2,1)} fusion(bf16[3,2,128,384]{3,2,1,0:T(8,128)(2,1)} %copy-done.6, bf16[1,2,128,384]{3,2,1,0:T(8,128)(2,1)S(1)} %fusion.48, bf16[1,2,128,384]{3,2,1,0:T(8,128)(2,1)} %bitcast.127, bf16[1,2,128,384]{3,2,1,0:T(8,128)(2,1)S(1)} %bitcast.125, bf16[256,2048]{1,0:T(8,128)(2,1)} %copy-done.1), kind=kOutput, calls=%fused_computation.4 | convolution fusion | flops 811597824 | bytes 4849664 | tf_op jit(solution)/shard_map/td,geth->edgh/dot_general | solution.py:84
  103.6 8.7 %copy.72 = bf16[2,1024,2,384]{3,2,1,0:T(2,128)(2,1)} copy(bf16[2,1024,2,384]{1,3,0,2:T(8,128)(2,1)} %convert_bitcast_fusion) | data formatting | bytes 6291456
  112.3 0.0 all-to-all-done
  112.3 1.4 %reduce_sum.23 = bf16[2,16,1024]{2,1,0:T(8,128)(2,1)S(1)} reduce(bf16[16,2,16,1024]{3,2,1,0:T(8,128)(2,1)} %all-to-all-done, bf16[]{:T(256)} %constant.23.clone.1), dimensions={0}, to_apply=%region_1.2 | reduce | flops 491520 | bytes 1114114 | tf_op jit(solution)/shard_map/reduce_sum | solution.py:82
  113.7 0.6 slice_bitcast_fusion.4
  (6 shorter events, 0.1 us)
Async XLA Ops:
  7.2 34.4 %copy-start = (bf16[2,2048,384]{2,1,0:T(8,128)(2,1)S(1)}, bf16[2,2048,384]{2,1,0:T(8,128)(2,1)}, u32[]{:S(2)}) copy-start(bf16[2,2048,384]{2,1,0:T(8,128)(2,1)} %param.10) | copy-start | bytes 9437188
  7.2 28.6 %all-gather.2.cloned.1.call-start = ((), (), s32[]{:S(2)}) async-start(), calls=%async_computation.1 | async-start | bytes 1216512 | tf_op jit(solution)/shard_map/all_gather | solution.py:32
  40.7 0.9 copy-start.4
  49.7 0.7 copy-start.2
  61.7 50.6 %all-to-all-start = ((bf16[16,2,16,1024]{3,2,1,0:T(8,128)(2,1)}), bf16[16,2,16,1024]{3,2,1,0:T(8,128)(2,1)}, u32[]{:S(2)}, u32[]{:S(2)}) async-start(bf16[16,2,16,1024]{3,2,1,0:T(8,128)(2,1)} %bitcast.121), calls=%async_computation | async-start | bytes 2097152 | tf_op jit(solution)/shard_map/all_to_all | solution.py:81
  66.1 3.0 %copy-start.5 = (f32[2,128,2,384]{3,1,2,0:T(8,128)S(1)}, f32[2,128,2,384]{3,1,2,0:T(8,128)}, u32[]{:S(2)}) copy-start(f32[2,128,2,384]{3,1,2,0:T(8,128)} %copy-done.4) | copy-start | bytes 2359300
  67.5 1.8 %copy-start.3 = (bf16[2,128,384]{2,1,0:T(8,128)(2,1)S(1)}, bf16[2,128,384]{2,1,0:T(8,128)(2,1)}, u32[]{:S(2)}) copy-start(bf16[2,128,384]{2,1,0:T(8,128)(2,1)} %copy-done.2) | copy-start | bytes 589828
  67.7 14.8 %collective-permute-start.1 = (bf16[128,2048]{1,0:T(8,128)(2,1)S(1)}, bf16[128,2048]{1,0:T(8,128)(2,1)S(1)}, u32[]{:S(2)}, u32[]{:S(2)}) collective-permute-start(bf16[128,2048]{1,0:T(8,128)(2,1)S(1)} %pad_maximum_fusion.3), channel_id=1, source_target_pairs={{0,16},{16,0},{1,17},{17,1},{2,18},{18,2},{3,19},{19,3},{4,20},{20... | collective-permute-start | bytes 1572872 | tf_op jit(solution)/shard_map/ppermute | solution.py:54
  69.4 25.1 %collective-permute-start = (bf16[3,2,128,384]{3,2,1,0:T(8,128)(2,1)S(1)}, bf16[3,2,128,384]{3,2,1,0:T(8,128)(2,1)S(1)}, u32[]{:S(2)}, u32[]{:S(2)}) collective-permute-start(bf16[3,2,128,384]{3,2,1,0:T(8,128)(2,1)S(1)} %pad_maximum_fusion.2), channel_id=1, source_target_pairs={{0,16},{16,0},{1,17},{17,1},{2,18},{18,2},{3,19},{19,3},{4,20},{20... | collective-permute-start | bytes 1769480 | tf_op jit(solution)/shard_map/ppermute | solution.py:54
  82.6 12.0 %copy-start.1 = (bf16[256,2048]{1,0:T(8,128)(2,1)}, bf16[256,2048]{1,0:T(8,128)(2,1)S(1)}, u32[]{:S(2)}) copy-start(bf16[256,2048]{1,0:T(8,128)(2,1)S(1)} %pad_maximum_fusion.1) | copy-start | bytes 3145732
  94.6 0.8 copy-start.6
Sparse Core Ops, SparseCore 0:
  10.8 24.9 all-gather.1
where the time goes:
time: 122 us; the launch traced here: 121 us
  waiting for transfers between devices  49.5 us (41%)
  local copies, waits for them, and re-layouts  25.9 us (21%)
  matrix products  19.3 us (16%)
  between operations  14.2 us (12%)
  starting transfers between devices  6.63 us (5%)
  other arithmetic  5.65 us (5%)
    all_gather x1, waiting for transfers between devices, body(): held = lax.all_gather(sent, 'expert', axis=0, tiled=True)  25.1 us
    ppermute x2, waiting for transfers between devices, moved(): lax.ppermute(value, 'dp', [(i, (i + shift) % n_dp) for i in range(n_dp)])  24.4 us
    unnamed x19, local copies, waits for them, and re-layouts  15.4 us
    another operation x4, local copies, waits for them, and re-layouts, body(): jnp.stack([out_part, in_part])  7.64 us
    dot_general x1, matrix products, body(): jnp.einsum('etgh,edgh->etd', pre_grads, weights_gate_up, preferred_elemen...  5.78 us
    all_to_all x1, starting transfers between devices, body(): lax.all_to_all(both, ('expert', 'tensor'), split_axis=0, concat_axis=0, t...  4.42 us
    dot_general x1, matrix products, body(): jnp.einsum('td,edgh->etgh', tok, weights_gate_up, preferred_element_type=...  3.95 us
    dot_general x1, matrix products, body(): jnp.einsum('td,geth->edgh', rows[:, :share], acts[:2], preferred_element_...  3.9 us
  transfers between devices with their start and end apart: 4, of which 3 were waited for; matrix products, arithmetic and copies ran while one was open for 15% of the time, Pallas kernels for 0%

commit v1 on v0

--- a/solution.py
+++ b/solution.py
@@ -5,6 +5,24 @@
 
 F32 = jnp.float32
 BF16 = jnp.bfloat16
+
+
+def in_order(pieces, dim):
+    pieces = jnp.moveaxis(pieces, 0, dim)
+    shape = pieces.shape
+    return pieces.reshape(*shape[:dim], shape[dim] * shape[dim + 1], *shape[dim + 2 :])
+
+
+def grow_blocks(x, axis):
+    peers = lax.axis_size(axis)
+    blocks = x[None]
+    for level in range(peers.bit_length() - 1):
+        distance = 1 << level
+        received = lax.ppermute(blocks, axis, [(i, i ^ distance) for i in range(peers)])
+        both = jnp.stack([blocks, received])
+        upper = lax.axis_index(axis) >> level & 1
+        blocks = jnp.where(upper == 0, both, both[::-1]).reshape(-1, *x.shape)
+    return blocks
 
 
 def cut(value):
@@ -29,7 +47,7 @@
     spare = -parts.shape[1] % 128
     parts = jnp.pad(parts, ((0, 0), (0, spare)))
     sent = jnp.concatenate([tokens, cotangent, parts], axis=1)
-    held = lax.all_gather(sent, "expert", axis=0, tiled=True)
+    held = in_order(grow_blocks(sent, "expert"), 0)
     tok = held[:, :width]
     cot = held[:, width : 2 * width]
     parts = held[:, 2 * width : 2 * width + 3 * expert_total].astype(F32)

time: 122 us -> 125 us (1.025)
  between operations: 14.2 us -> 0.84 us
  starting transfers between devices: 6.63 us -> 14.1 us
  waiting for transfers between devices: 49.5 us -> 56.3 us
  other arithmetic: 5.65 us -> 9.22 us
  local copies, waits for them, and re-layouts: 25.9 us -> 24.5 us
    ppermute x0 -> x3, waiting for transfers between devices: none -> 32 us  [grow_blocks(): lax.ppermute(blocks, axis, [(i, i ^ distance) for i in range(peers)])]
    all_gather x1 -> x0, waiting for transfers between devices: 25.1 us -> none  [body(): held = lax.all_gather(sent, 'expert', axis=0, tiled=True)]
    ppermute x0 -> x3, starting transfers between devices: none -> 6.21 us  [grow_blocks(): lax.ppermute(blocks, axis, [(i, i ^ distance) for i in range(peers)])]
    another operation x1 -> x6, other arithmetic: 0.01 us -> 4.02 us  [the longest x5 4.02 us: grow_blocks(): both = jnp.stack([blocks, received])]
    concatenate x1 -> x0, other arithmetic: 1.54 us -> none  [body(): sent = jnp.concatenate([tokens, cotangent, parts], axis=1)]
    all_to_all x1, starting transfers between devices: 4.42 us -> 5.73 us  [body(): lax.all_to_all(both, ('expert', 'tensor'), split_axis=0, concat_axis=0, t...]
    unnamed x19 -> x21, local copies, waits for them, and re-layouts: 15.4 us -> 14.9 us
  transfers between devices with their start and end apart: 4 -> 6, of which waited for: 3 -> 5; matrix products, arithmetic and copies ran while one was open for 15% -> 15% of each run, Pallas kernels for 0% -> 0%
where the time goes in v1:
time: 125 us; the launch traced here: 124 us
  waiting for transfers between devices  56.3 us (45%)
  local copies, waits for them, and re-layouts  24.5 us (20%)
  matrix products  19.4 us (16%)
  starting transfers between devices  14.1 us (11%)
  other arithmetic  9.22 us (7%)
    ppermute x3, waiting for transfers between devices, grow_blocks(): lax.ppermute(blocks, axis, [(i, i ^ distance) for i in range(peers)])  32 us
    ppermute x2, waiting for transfers between devices, moved(): lax.ppermute(value, 'dp', [(i, (i + shift) % n_dp) for i in range(n_dp)])  24.3 us
    unnamed x21, local copies, waits for them, and re-layouts  14.9 us
    another operation x4, local copies, waits for them, and re-layouts, body(): jnp.stack([out_part, in_part])  7.58 us
    ppermute x3, starting transfers between devices, grow_blocks(): lax.ppermute(blocks, axis, [(i, i ^ distance) for i in range(peers)])  6.21 us
    dot_general x1, matrix products, body(): jnp.einsum('etgh,edgh->etd', pre_grads, weights_gate_up, preferred_elemen...  5.8 us
    all_to_all x1, starting transfers between devices, body(): lax.all_to_all(both, ('expert', 'tensor'), split_axis=0, concat_axis=0, t...  5.73 us
    another operation x5, other arithmetic, grow_blocks(): both = jnp.stack([blocks, received])  4.02 us
  transfers between devices with their start and end apart: 6, of which 5 were waited for; matrix products, arithmetic and copies ran while one was open for 15% of the time, Pallas kernels for 0%

profile of v1, /device:TPU:0, one launch (start us, length us, event | category | flops | bytes accessed | tf_op | source)
XLA Modules:
  0.0 124.4 jit_solution(9240159644654613246)
XLA Ops:
  0.6 0.0 copy-start
  0.6 0.9 copy.60
  1.6 0.8 copy.61
  2.4 0.1 select_reduce_fusion
  2.5 0.1 fusion.60
  2.6 0.9 fusion.54
  3.5 0.5 collective-permute-start
  4.0 1.0 collective-permute-done
  5.0 0.8 fusion.50
  5.8 2.9 %collective-permute-start.1 = (bf16[2,16,4224]{2,1,0:T(8,128)(2,1)}, bf16[2,16,4224]{2,1,0:T(8,128)(2,1)}, u32[]{:S(2)}, u32[]{:S(2)}) collective-permute-start(bf16[2,16,4224]{2,1,0:T(8,128)(2,1)} %get-tuple-element.33), channel_id=1, source_target_pairs={{0,4},{2,6},{4,0},{6,2},{8,12},{10,14},{12,8},{14,10},{1,5},{3,7},... | collective-permute-start | bytes 811016 | tf_op jit(solution)/shard_map/ppermute | solution.py:21
  8.7 7.1 %collective-permute-done.1 = bf16[2,16,4224]{2,1,0:T(8,128)(2,1)} collective-permute-done((bf16[2,16,4224]{2,1,0:T(8,128)(2,1)}, bf16[2,16,4224]{2,1,0:T(8,128)(2,1)}, u32[]{:S(2)}, u32[]{:S(2)}) %collective-permute-start.1) | collective-permute-done | bytes 270368 | tf_op jit(solution)/shard_map/ppermute | solution.py:21
  15.8 1.0 pad_maximum_fusion.4
  16.8 0.9 reverse_select_fusion.1
  17.7 2.8 %collective-permute-start.2 = (bf16[4,16,4224]{2,1,0:T(8,128)(2,1)}, bf16[4,16,4224]{2,1,0:T(8,128)(2,1)}, u32[]{:S(2)}, u32[]{:S(2)}) collective-permute-start(bf16[4,16,4224]{2,1,0:T(8,128)(2,1)} %bitcast.7), channel_id=1, source_target_pairs={{0,8},{2,10},{4,12},{6,14},{8,0},{10,2},{12,4},{14,6},{1,9},{3,11}... | collective-permute-start | bytes 1622024 | tf_op jit(solution)/shard_map/ppermute | solution.py:21
  20.5 23.9 %collective-permute-done.2 = bf16[4,16,4224]{2,1,0:T(8,128)(2,1)} collective-permute-done((bf16[4,16,4224]{2,1,0:T(8,128)(2,1)}, bf16[4,16,4224]{2,1,0:T(8,128)(2,1)}, u32[]{:S(2)}, u32[]{:S(2)}) %collective-permute-start.2) | collective-permute-done | bytes 540704 | tf_op jit(solution)/shard_map/ppermute | solution.py:21
  44.3 1.3 %pad_maximum_fusion = bf16[2,4,16,4224]{3,2,1,0:T(8,128)(2,1)S(1)} fusion(bf16[1,4,16,4224]{3,2,1,0:T(8,128)(2,1)} %bitcast.8, bf16[1,4,16,4224]{3,2,1,0:T(8,128)(2,1)} %bitcast.6), kind=kLoop, calls=%fused_computation.22 | loop fusion | flops 540672 | bytes 2162688 | tf_op jit(solution)/shard_map/stack | solution.py:22
  45.7 0.2 reverse_select_fusion
  45.8 0.0 copy-start.1
  45.9 1.0 copy-done.1
  46.8 0.1 copy.78
  46.9 4.0 %fusion.12 = f32[2,128,2,384]{3,1,2,0:T(8,128)S(1)} fusion(bf16[2,2048,2,384]{3,2,1,0:T(2,128)(2,1)} %param.9, bf16[128,4224]{1,0:T(8,128)(2,1)} %bitcast.136), kind=kOutput, calls=%fused_computation.12 | convolution fusion | flops 805306368 | bytes 7602176 | tf_op jit(solution)/shard_map/td,edgh->etgh/dot_general | solution.py:75
  50.9 0.0 copy-start.5
  50.9 2.0 %fusion.44 = (bf16[2,128,384]{2,1,0:T(8,128)(2,1)S(1)}, bf16[2,128,384]{2,1,0:T(8,128)(2,1)S(1)}) fusion(f32[2,128,2,384]{3,1,2,0:T(8,128)S(1)} %fusion.12, bf16[2,2048,384]{2,1,0:T(8,128)(2,1)S(1)} %copy-done, bf16[128,4224]{1,0:T(8,128)(2,1)} %bitcast.137, f32[2,128]{1,0:T(2,128)S(1)} %fusion.62), kind=kOutput, calls=%fused_computation.59 | convolution fusion | flops 404029440 | bytes 4850688 | tf_op jit(solution)/shard_map/td,edh->eth/dot_general | solution.py:81
  52.9 1.9 %fusion.7 = bf16[128,2048]{1,0:T(8,128)(2,1)} fusion(bf16[2,2048,384]{2,1,0:T(8,128)(2,1)S(1)} %copy-done, f32[2,128,2,384]{3,1,2,0:T(8,128)S(1)} %fusion.12, f32[2,128]{1,0:T(2,128)S(1)} %fusion.62), kind=kOutput, calls=%fused_computation.7 | convolution fusion | flops 403603456 | bytes 4457472 | tf_op jit(solution)/shard_map/eth,edh->etd/dot_general | solution.py:88
  54.9 2.2 %stack.52 = bf16[1,8,16,2,1024]{4,3,2,1,0:T(2,128)(2,1)} reshape(bf16[128,2048]{1,0:T(8,128)(2,1)} %fusion.7) | data formatting | bytes 1048576 | tf_op jit(solution)/shard_map/stack | solution.py:93
  57.1 2.0 %copy.66 = bf16[1,8,16,2,1024]{4,2,0,3,1:T(8,128)(2,1)} copy(bf16[1,8,16,2,1024]{4,3,2,1,0:T(2,128)(2,1)} %stack.52) | data formatting | bytes 1048576 | tf_op jit(solution)/shard_map/stack | solution.py:93
  59.1 5.8 %fusion.8 = bf16[128,2048]{1,0:T(8,128)(2,1)} fusion(bf16[2,2048,2,384]{3,2,1,0:T(2,128)(2,1)} %param.9, bf16[2,128,1,384]{3,1,0,2:T(8,128)(2,1)S(1)} %bitcast.144, bf16[2,128,1,384]{3,1,0,2:T(8,128)(2,1)S(1)} %bitcast.140), kind=kOutput, calls=%fused_computation.8 | convolution fusion | flops 805765120 | bytes 7208960 | tf_op jit(solution)/shard_map/etgh,edgh->etd/dot_general | solution.py:91
  64.9 2.2 %stack.56 = bf16[1,8,16,2,1024]{4,3,2,1,0:T(2,128)(2,1)} reshape(bf16[128,2048]{1,0:T(8,128)(2,1)} %fusion.8) | data formatting | bytes 1048576 | tf_op jit(solution)/shard_map/stack | solution.py:93
  67.1 1.2 copy.67
  68.3 2.2 %pad_maximum_fusion.1 = bf16[2,8,16,2,1024]{4,2,0,3,1:T(8,128)(2,1)} fusion(bf16[1,8,16,2,1024]{4,2,0,3,1:T(8,128)(2,1)S(1)} %copy.67, bf16[1,8,16,2,1024]{4,2,0,3,1:T(8,128)(2,1)} %copy.66), kind=kLoop, calls=%fused_computation.23 | loop fusion | flops 524288 | bytes 2097152 | tf_op jit(solution)/shard_map/stack | solution.py:93
  70.4 5.7 %all-to-all-start = ((bf16[16,2,16,1024]{3,2,1,0:T(8,128)(2,1)}), bf16[16,2,16,1024]{3,2,1,0:T(8,128)(2,1)}, u32[]{:S(2)}, u32[]{:S(2)}) async-start(bf16[16,2,16,1024]{3,2,1,0:T(8,128)(2,1)} %bitcast.139), calls=%async_computation | async-start | bytes 2097152 | tf_op jit(solution)/shard_map/all_to_all | solution.py:99
  76.2 0.0 copy-start.6
  76.2 1.3 %fusion.70 = (bf16[128,2048]{1,0:T(8,128)(2,1)S(1)}, bf16[128,2048]{1,0:T(8,128)(2,1)S(1)}) fusion(bf16[128,4224]{1,0:T(8,128)(2,1)} %bitcast.138), kind=kLoop, calls=%fused_computation.105 | loop fusion | bytes 2097152 | tf_op jit(solution)/shard_map/slice | solution.py:51
  77.6 0.1 constant_dynamic-slice_fusion.4
  77.7 1.6 %collective-permute-start.4 = (bf16[128,2048]{1,0:T(8,128)(2,1)S(1)}, bf16[128,2048]{1,0:T(8,128)(2,1)S(1)}, u32[]{:S(2)}, u32[]{:S(2)}) collective-permute-start(bf16[128,2048]{1,0:T(8,128)(2,1)S(1)} %pad_maximum_fusion.5), channel_id=1, source_target_pairs={{0,16},{16,0},{1,17},{17,1},{2,18},{18,2},{3,19},{19,3},{4,20},{20... | collective-permute-start | bytes 1572872 | tf_op jit(solution)/shard_map/ppermute | solution.py:72
  79.3 0.1 fusion.48
  79.4 0.1 pad_maximum_fusion.3
  79.5 0.6 collective-permute-start.3
  80.1 12.4 %collective-permute-done.4 = bf16[128,2048]{1,0:T(8,128)(2,1)S(1)} collective-permute-done((bf16[128,2048]{1,0:T(8,128)(2,1)S(1)}, bf16[128,2048]{1,0:T(8,128)(2,1)S(1)}, u32[]{:S(2)}, u32[]{:S(2)}) %collective-permute-start.4) | collective-permute-done | bytes 524320 | tf_op jit(solution)/shard_map/ppermute | solution.py:72
  92.5 0.1 pad_maximum_fusion.2
  92.6 12.0 %collective-permute-done.3 = bf16[3,2,128,384]{3,2,1,0:T(8,128)(2,1)S(1)} collective-permute-done((bf16[3,2,128,384]{3,2,1,0:T(8,128)(2,1)S(1)}, bf16[3,2,128,384]{3,2,1,0:T(8,128)(2,1)S(1)}, u32[]{:S(2)}, u32[]{:S(2)}) %collective-permute-start.3) | collective-permute-done | bytes 589856 | tf_op jit(solution)/shard_map/ppermute | solution.py:72
  104.6 0.8 copy-done.7
  105.4 1.8 %fusion.11 = bf16[2,1024,384]{1,2,0:T(8,128)(2,1)} fusion(bf16[256,2048]{1,0:T(8,128)(2,1)S(1)} %pad_maximum_fusion.2, bf16[3,2,128,384]{3,2,1,0:T(8,128)(2,1)S(1)} %collective-permute-done.3, bf16[1,2,128,384]{3,2,1,0:T(8,128)(2,1)S(1)} %fusion.48, bf16[1,2,128,384]{3,2,1,0:T(8,128)(2,1)S(1)} %bitcast.147, bf16[1,2,128,384]{3,2,1,0:T(8,128)(2,1)S(1)} %bitcast.142), kind=kOutput, calls=%fused_computation.11 | convolution fusion | flops 405012480 | bytes 3276800 | tf_op jit(solution)/shard_map/td,eth->edh/dot_general | solution.py:105
  107.2 2.6 %copy.71 = bf16[2,1024,384]{2,1,0:T(8,128)(2,1)} copy(bf16[2,1024,384]{1,2,0:T(8,128)(2,1)} %fusion.11) | data formatting | bytes 3145728
  109.7 3.9 %convert_bitcast_fusion = bf16[2,1024,2,384]{1,3,0,2:T(8,128)(2,1)} fusion(bf16[3,2,128,384]{3,2,1,0:T(8,128)(2,1)} %copy-done.7, bf16[1,2,128,384]{3,2,1,0:T(8,128)(2,1)S(1)} %fusion.48, bf16[1,2,128,384]{3,2,1,0:T(8,128)(2,1)} %bitcast.145, bf16[1,2,128,384]{3,2,1,0:T(8,128)(2,1)S(1)} %bitcast.143, bf16[256,2048]{1,0:T(8,128)(2,1)} %copy-done.2), kind=kOutput, calls=%fused_computation.4 | convolution fusion | flops 811597824 | bytes 4849664 | tf_op jit(solution)/shard_map/td,geth->edgh/dot_general | solution.py:102
  113.7 8.7 %copy.70 = bf16[2,1024,2,384]{3,2,1,0:T(2,128)(2,1)} copy(bf16[2,1024,2,384]{1,3,0,2:T(8,128)(2,1)} %convert_bitcast_fusion) | data formatting | bytes 6291456
  122.3 1.4 %reduce_sum.23 = bf16[2,16,1024]{2,1,0:T(8,128)(2,1)S(1)} reduce(bf16[16,2,16,1024]{3,2,1,0:T(8,128)(2,1)} %all-to-all-done, bf16[]{:T(256)} %constant.28.clone.1), dimensions={0}, to_apply=%region_1.2 | reduce | flops 491520 | bytes 1114114 | tf_op jit(solution)/shard_map/reduce_sum | solution.py:100
  123.8 0.6 slice_bitcast_fusion.4
  (17 shorter events, 0.1 us)
Async XLA Ops:
  0.6 50.3 %copy-start = (bf16[2,2048,384]{2,1,0:T(8,128)(2,1)S(1)}, bf16[2,2048,384]{2,1,0:T(8,128)(2,1)}, u32[]{:S(2)}) copy-start(bf16[2,2048,384]{2,1,0:T(8,128)(2,1)} %param.10) | copy-start | bytes 9437188
  3.5 1.5 %collective-permute-start = (bf16[1,16,4224]{2,1,0:T(8,128)(2,1)S(1)}, bf16[1,16,4224]{2,1,0:T(8,128)(2,1)S(1)}, u32[]{:S(2)}, u32[]{:S(2)}) collective-permute-start(bf16[1,16,4224]{2,1,0:T(8,128)(2,1)S(1)} %get-tuple-element.35), channel_id=1, source_target_pairs={{0,2},{2,0},{4,6},{6,4},{8,10},{10,8},{12,14},{14,12},{1,3},{3,1},... | collective-permute-start | bytes 405512 | tf_op jit(solution)/shard_map/ppermute | solution.py:21
  5.8 10.0 %collective-permute-start.1 = (bf16[2,16,4224]{2,1,0:T(8,128)(2,1)}, bf16[2,16,4224]{2,1,0:T(8,128)(2,1)}, u32[]{:S(2)}, u32[]{:S(2)}) collective-permute-start(bf16[2,16,4224]{2,1,0:T(8,128)(2,1)} %get-tuple-element.33), channel_id=1, source_target_pairs={{0,4},{2,6},{4,0},{6,2},{8,12},{10,14},{12,8},{14,10},{1,5},{3,7},... | collective-permute-start | bytes 811016 | tf_op jit(solution)/shard_map/ppermute | solution.py:21
  17.7 26.6 %collective-permute-start.2 = (bf16[4,16,4224]{2,1,0:T(8,128)(2,1)}, bf16[4,16,4224]{2,1,0:T(8,128)(2,1)}, u32[]{:S(2)}, u32[]{:S(2)}) collective-permute-start(bf16[4,16,4224]{2,1,0:T(8,128)(2,1)} %bitcast.7), channel_id=1, source_target_pairs={{0,8},{2,10},{4,12},{6,14},{8,0},{10,2},{12,4},{14,6},{1,9},{3,11}... | collective-permute-start | bytes 1622024 | tf_op jit(solution)/shard_map/ppermute | solution.py:21
  45.8 1.0 copy-start.1
  50.9 2.0 %copy-start.5 = (f32[2,128,2,384]{3,1,2,0:T(8,128)}, f32[2,128,2,384]{3,1,2,0:T(8,128)S(1)}, u32[]{:S(2)}) copy-start(f32[2,128,2,384]{3,1,2,0:T(8,128)S(1)} %fusion.12) | copy-start | bytes 2359300
  52.9 6.1 %copy-start.3 = (bf16[2,128,384]{2,1,0:T(8,128)(2,1)}, bf16[2,128,384]{2,1,0:T(8,128)(2,1)S(1)}, u32[]{:S(2)}) copy-start(bf16[2,128,384]{2,1,0:T(8,128)(2,1)S(1)} %get-tuple-element.25) | copy-start | bytes 589828
  70.4 51.9 %all-to-all-start = ((bf16[16,2,16,1024]{3,2,1,0:T(8,128)(2,1)}), bf16[16,2,16,1024]{3,2,1,0:T(8,128)(2,1)}, u32[]{:S(2)}, u32[]{:S(2)}) async-start(bf16[16,2,16,1024]{3,2,1,0:T(8,128)(2,1)} %bitcast.139), calls=%async_computation | async-start | bytes 2097152 | tf_op jit(solution)/shard_map/all_to_all | solution.py:99
  76.2 3.1 %copy-start.6 = (f32[2,128,2,384]{3,1,2,0:T(8,128)S(1)}, f32[2,128,2,384]{3,1,2,0:T(8,128)}, u32[]{:S(2)}) copy-start(f32[2,128,2,384]{3,1,2,0:T(8,128)} %copy-done.5) | copy-start | bytes 2359300
  77.5 1.9 %copy-start.4 = (bf16[2,128,384]{2,1,0:T(8,128)(2,1)S(1)}, bf16[2,128,384]{2,1,0:T(8,128)(2,1)}, u32[]{:S(2)}) copy-start(bf16[2,128,384]{2,1,0:T(8,128)(2,1)} %copy-done.3) | copy-start | bytes 589828
  77.7 14.8 %collective-permute-start.4 = (bf16[128,2048]{1,0:T(8,128)(2,1)S(1)}, bf16[128,2048]{1,0:T(8,128)(2,1)S(1)}, u32[]{:S(2)}, u32[]{:S(2)}) collective-permute-start(bf16[128,2048]{1,0:T(8,128)(2,1)S(1)} %pad_maximum_fusion.5), channel_id=1, source_target_pairs={{0,16},{16,0},{1,17},{17,1},{2,18},{18,2},{3,19},{19,3},{4,20},{20... | collective-permute-start | bytes 1572872 | tf_op jit(solution)/shard_map/ppermute | solution.py:72
  79.5 25.1 %collective-permute-start.3 = (bf16[3,2,128,384]{3,2,1,0:T(8,128)(2,1)S(1)}, bf16[3,2,128,384]{3,2,1,0:T(8,128)(2,1)S(1)}, u32[]{:S(2)}, u32[]{:S(2)}) collective-permute-start(bf16[3,2,128,384]{3,2,1,0:T(8,128)(2,1)S(1)} %pad_maximum_fusion.3), channel_id=1, source_target_pairs={{0,16},{16,0},{1,17},{17,1},{2,18},{18,2},{3,19},{19,3},{4,20},{20... | collective-permute-start | bytes 1769480 | tf_op jit(solution)/shard_map/ppermute | solution.py:72
  92.6 12.0 %copy-start.2 = (bf16[256,2048]{1,0:T(8,128)(2,1)}, bf16[256,2048]{1,0:T(8,128)(2,1)S(1)}, u32[]{:S(2)}) copy-start(bf16[256,2048]{1,0:T(8,128)(2,1)S(1)} %pad_maximum_fusion.2) | copy-start | bytes 3145732
  104.6 0.8 copy-start.7
